TPU v7x, 256 devices: a whole 4x4x8 slice. The times are simulated.
256 devices in a mesh: ctx: 8 (over x, core), exp: 32 (over y, z).
Axes of the slice: x: 4, y: 4, z: 8, core: 2. Of those that a mesh axis runs over, the one named last changes fastest.
Arguments:
- tokens_in: bfloat16 [1024, 6144], P('ctx'), may hold values from -6 to 6
- queries: bfloat16 [1024, 8192], P('ctx', 'exp'), may hold values from -6 to 6
- keys: bfloat16 [1024, 8192], P('ctx', 'exp'), may hold values from -6 to 6
- values: bfloat16 [1024, 8192], P('ctx', 'exp'), may hold values from -6 to 6
- log_decay: float32 [64, 1024], P('exp', 'ctx'), may hold values from -1.3 to 0
- incoming_state: float32 [64, 128, 128], P('exp'), may hold values from -12 to 12
- attn_gain: float32 [8192], P('exp'), may hold values from 0.1 to 1.9
- w_out: bfloat16 [8192, 6144], P('exp'), may hold values from -0.0625 to 0.0625
- ffn_gain: float32 [6144], replicated, may hold values from 0.1 to 1.9
- router: bfloat16 [6144, 4], replicated, may hold values from -0.078125 to 0.078125
- expert_ids: int32 [1024, 2], P('ctx'), may hold values from 0 to 3, all different within a row; in each aligned block of 128 rows (0 to 127, 128 to 255, ...) at most 80 rows name the same one
- w_in: bfloat16 [2, 36864, 6144], P(None, ('exp', 'ctx')), may hold values from -0.078125 to 0.078125
- w_down: bfloat16 [36864, 6144], P(('exp', 'ctx')), may hold values from -0.0625 to 0.0625
Outputs:
- mixed: bfloat16 [1024, 6144], P('ctx', 'exp')
Inputs may be any that keep to these rules, and one draw needn't show every extreme that they name: `expert_ids`: A token's two experts differ. Among the 128 tokens of one index of ctx no expert is named by more than 80 tokens, a bound that some block reaches of them.
All inputs are finite; a program needn't handle non-finite values.
Results may differ from a plain program's by a relative error of at most 0.027.
Values may be sent and summed in bfloat16 or wider, within the bound.
A program may use at most 128 MiB of HBM per device.

v0:
```python
import jax
import jax.numpy as jnp
from jax import lax
from jax.sharding import PartitionSpec as P

FF = 9216
CAP = 80
HIGHEST = lax.Precision.HIGHEST
epsilon = 1e-06


def shifted(value, axis, steps):
    count = lax.axis_size(axis)
    initial, last = (max(0, -steps), min(count, count - steps))
    return lax.ppermute(value, axis, [(source, source + steps) for source in range(initial, last)])


def rms_scale(values_f32, gain):
    mean_square = jnp.mean(values_f32 * values_f32, axis=-1, keepdims=True)
    return values_f32 * lax.rsqrt(mean_square + epsilon) * gain


def local(
    tokens_in,
    queries,
    keys,
    values,
    log_decay,
    incoming_state,
    attn_gain,
    w_out,
    ffn_gain,
    router,
    expert_ids,
    w_in,
    w_down,
):
    row_count = queries.shape[0]
    head_count = incoming_state.shape[0]
    head_size = incoming_state.shape[1]
    scale = head_size ** (-0.5)
    q_heads = queries.reshape(row_count, head_count, head_size)
    k_heads = keys.reshape(row_count, head_count, head_size)
    v_float = values.reshape(row_count, head_count, head_size).astype(jnp.float32)
    cumulative = jnp.cumsum(log_decay, axis=1)
    decay_total = jnp.exp(cumulative[:, -1])
    tail = jnp.exp(cumulative[:, -1:] - cumulative)
    key_scaled = k_heads.astype(jnp.float32) * tail.T[:, :, None]
    local_state = jnp.einsum("thd,the->hde", key_scaled, v_float, precision=HIGHEST)
    leading = lax.axis_index("ctx") == 0
    state_in = jnp.where(leading, incoming_state, jnp.zeros_like(incoming_state))
    for hop_index in range(lax.axis_size("ctx") - 1):
        outgoing = decay_total[:, None, None] * state_in + local_state
        arrived = shifted(outgoing.astype(jnp.bfloat16), "ctx", 1).astype(outgoing.dtype)
        state_in = jnp.where(leading, incoming_state, arrived)
    positions = lax.iota(jnp.int32, row_count)
    lower = (positions[:, None] >= positions[None, :])[None, :, :]
    gap = jnp.where(lower, cumulative[:, :, None] - cumulative[:, None, :], 0.0)
    weight = jnp.where(lower, jnp.exp(gap), 0.0)
    scores = (
        jnp.einsum("thd,shd->hts", q_heads, k_heads, preferred_element_type=jnp.float32)
        * scale
        * weight
    )
    query_scaled = q_heads.astype(jnp.float32) * (scale * jnp.exp(cumulative)).T[:, :, None]
    attended = jnp.einsum("hts,she->the", scores, v_float, precision=HIGHEST) + jnp.einsum(
        "thd,hde->the", query_scaled, state_in, precision=HIGHEST
    )
    attn_heads = (
        rms_scale(attended, attn_gain.reshape(head_count, head_size))
        .astype(jnp.bfloat16)
        .reshape(row_count, head_count * head_size)
    )
    width = tokens_in.shape[1]
    exp_count = lax.axis_size("exp")
    attn_full = lax.psum(
        jnp.dot(attn_heads, w_out, preferred_element_type=jnp.float32).astype(jnp.bfloat16), "exp"
    ).astype(jnp.float32)
    mid_full = tokens_in.astype(jnp.float32) + attn_full
    normed = rms_scale(mid_full, ffn_gain).astype(jnp.bfloat16)
    expert_count = router.shape[1]
    logits = jnp.dot(normed, router, preferred_element_type=jnp.float32)
    picked = expert_ids[:, :, None] == lax.iota(jnp.int32, expert_count)[None, None, :]
    chosen = jnp.sum(jnp.where(picked, logits[:, None, :], 0.0), axis=2)
    sigmoid_gate = jax.nn.sigmoid(chosen)
    gates = sigmoid_gate / jnp.sum(sigmoid_gate, axis=1, keepdims=True)
    slice_units = w_in.shape[1]
    block_index = lax.axis_index("exp") * lax.axis_size("ctx") + lax.axis_index("ctx")
    owned = block_index * slice_units // FF
    paired = w_in.reshape(2 * slice_units, width)
    flat_routes = expert_ids.reshape(row_count * 2)
    one_hot = (flat_routes[:, None] == lax.iota(jnp.int32, expert_count)[None, :]).astype(jnp.int32)
    earlier_count = jnp.cumsum(one_hot, axis=0) - one_hot
    slot_of = jnp.sum(earlier_count * one_hot, axis=1).reshape(row_count, 2)
    capacity = CAP
    in_slot = (expert_ids == owned)[:, :, None] & (
        slot_of[:, :, None] == lax.iota(jnp.int32, capacity)[None, None, :]
    )
    placement = jnp.any(in_slot, axis=1).T.astype(jnp.bfloat16)
    slot_buffer = jnp.dot(placement, normed, preferred_element_type=jnp.float32).astype(
        jnp.bfloat16
    )
    combine = jnp.sum(jnp.where(in_slot, gates[:, :, None], 0.0), axis=1)
    projected = lax.dot_general(
        lax.all_gather(slot_buffer, "ctx", axis=0, tiled=True),
        paired,
        (((1,), (1,)), ((), ())),
        preferred_element_type=jnp.float32,
    )
    hidden = (jax.nn.silu(projected[:, :slice_units]) * projected[:, slice_units:]).astype(
        jnp.bfloat16
    )
    partials = jnp.dot(hidden, w_down, preferred_element_type=jnp.float32).astype(jnp.bfloat16)
    summed = lax.psum_scatter(
        partials.astype(jnp.float32).astype(jnp.bfloat16), "ctx", scatter_dimension=0, tiled=True
    ).astype(jnp.float32)
    contrib = jnp.dot(combine, summed, precision=HIGHEST)
    column_count = width // exp_count
    column_start = lax.axis_index("exp") * column_count
    residual = lax.dynamic_slice_in_dim(mid_full, column_start, column_count, 1)
    total = lax.psum_scatter(
        contrib.astype(jnp.bfloat16), "exp", scatter_dimension=1, tiled=True
    ).astype(jnp.float32)
    return (total + residual).astype(jnp.bfloat16)


def solution(mesh):
    return jax.shard_map(
        local,
        mesh=mesh,
        in_specs=(
            P("ctx", None),
            P("ctx", "exp"),
            P("ctx", "exp"),
            P("ctx", "exp"),
            P("exp", "ctx"),
            P("exp", None, None),
            P("exp"),
            P("exp", None),
            P(),
            P(),
            P("ctx", None),
            P(None, ("exp", "ctx"), None),
            P(("exp", "ctx"), None),
        ),
        out_specs=P("ctx", "exp"),
        check_vma=False,
    )
```

profile of v0, /device:TPU:2, one launch (start us, length us, event | category | flops | bytes accessed | tf_op | source)
XLA Modules:
  0.0 555.5 jit_solution(10375486550913919019)
XLA Ops:
  10.8 1.9 collective-permute-start
  12.7 3.7 collective-permute-done
  16.4 1.9 collective-permute-start.1
  18.4 3.7 collective-permute-done.1
  22.1 1.9 collective-permute-start.2
  24.0 3.7 collective-permute-done.2
  27.8 1.9 collective-permute-start.3
  29.7 3.7 collective-permute-done.3
  33.5 1.9 collective-permute-start.4
  35.4 3.6 collective-permute-done.4
  39.1 1.9 collective-permute-start.5
  42.1 2.6 collective-permute-done.5
  44.8 1.9 collective-permute-start.6
  47.9 2.5 collective-permute-done.6
  61.9 145.4 %all-reduce.2.cloned.1.call-done = bf16[128,6144]{1,0:T(8,128)(2,1)} async-done(((bf16[128,6144]{1,0:T(8,128)(2,1)}), bf16[128,6144]{1,0:T(8,128)(2,1)}) %all-reduce.2.cloned.1.call-update) | async-done | bytes 1572880 | tf_op jit(solution)/shard_map/psum | solution.py:76
  207.3 4.3 multiply_reduce_fusion
  212.2 1.9 convolution_convert_fusion.3
  214.1 46.6 %all-gather.2.cloned.1.call-done = bf16[640,6144]{1,0:T(8,128)(2,1)} async-done(((bf16[80,6144]{1,0:T(8,128)(2,1)}), bf16[640,6144]{1,0:T(8,128)(2,1)}) %all-gather.2.cloned.1.call-update) | async-done | bytes 7864336 | tf_op jit(solution)/shard_map/all_gather | solution.py:105
  260.7 5.4 fusion.31
  266.1 5.4 convolution_convert_fusion
  271.6 2.6 fusion.30
  274.9 47.8 %reduce-scatter.5.cloned.1.call-done = bf16[80,6144]{1,0:T(8,128)(2,1)} async-done(((bf16[640,6144]{1,0:T(8,128)(2,1)}), bf16[80,6144]{1,0:T(8,128)(2,1)}) %reduce-scatter.5.cloned.1.call-update) | async-done | bytes 983056 | tf_op jit(solution)/shard_map/reduce_scatter | solution.py:114
  322.7 4.1 fusion
  326.9 217.3 %reduce-scatter.7.cloned.1.call-done = bf16[192,128]{1,0:T(8,128)(2,1)} async-done(((bf16[6144,128]{1,0:T(8,128)(2,1)}), bf16[192,128]{1,0:T(8,128)(2,1)}) %reduce-scatter.7.cloned.1.call-update) | async-done | bytes 49168
  (79 shorter events, 24.4 us)
Async XLA Ops:
  6.5 254.1 %copy-start = (bf16[2,144,6144]{2,1,0:T(8,128)(2,1)S(1)}, bf16[2,144,6144]{2,1,0:T(8,128)(2,1)}, u32[]{:S(2)}) copy-start(bf16[2,144,6144]{2,1,0:T(8,128)(2,1)} %param.24) | copy-start | bytes 10616836
  6.5 200.8 %all-reduce.2.cloned.1.call-start = ((), (), s32[]{:S(2)}) async-start(), calls=%async_computation.2 | async-start | bytes 3145728 | tf_op jit(solution)/shard_map/psum | solution.py:76
  9.5 40.9 %copy-start.1 = (f32[2,128,128]{2,1,0:T(8,128)S(1)}, f32[2,128,128]{2,1,0:T(8,128)}, u32[]{:S(2)}) copy-start(f32[2,128,128]{2,1,0:T(8,128)} %param.18) | copy-start | bytes 393220
  9.5 40.9 %copy-start.6 = (bf16[128,256]{1,0:T(8,128)(2,1)S(1)}, bf16[128,256]{1,0:T(8,128)(2,1)}, u32[]{:S(2)}) copy-start(bf16[128,256]{1,0:T(8,128)(2,1)} %param.14) | copy-start | bytes 196612
  9.5 41.4 %copy-start.12 = (f32[256]{0:T(256)S(1)}, f32[256]{0:T(256)}, u32[]{:S(2)}) copy-start(f32[256]{0:T(256)} %param.19) | copy-start | bytes 3076
  9.5 41.5 %copy-start.4 = (bf16[256,6144]{1,0:T(8,128)(2,1)S(1)}, bf16[256,6144]{1,0:T(8,128)(2,1)}, u32[]{:S(2)}) copy-start(bf16[256,6144]{1,0:T(8,128)(2,1)} %param.20) | copy-start | bytes 9437188
  10.8 5.6 %collective-permute-start = (bf16[2,128,128]{2,1,0:T(8,128)(2,1)S(1)}, bf16[2,128,128]{2,1,0:T(8,128)(2,1)S(1)}, u32[]{:S(2)}, u32[]{:S(2)}) collective-permute-start(bf16[2,128,128]{2,1,0:T(8,128)(2,1)S(1)} %get-tuple-element.9), channel_id=1, source_target_pairs={{0,32},{32,64},{64,96},{96,128},{128,160},{160,192},{192,224},{1,3... | collective-permute-start | bytes 196616 | tf_op jit(solution)/shard_map/ppermute | solution.py:15
  16.4 5.6 %collective-permute-start.1 = (bf16[2,128,128]{2,1,0:T(8,128)(2,1)S(1)}, bf16[2,128,128]{2,1,0:T(8,128)(2,1)S(1)}, u32[]{:S(2)}, u32[]{:S(2)}) collective-permute-start(bf16[2,128,128]{2,1,0:T(8,128)(2,1)S(1)} %add_convert_fusion.6), channel_id=1, source_target_pairs={{0,32},{32,64},{64,96},{96,128},{128,160},{160,192},{192,224},{1,3... | collective-permute-start | bytes 196616 | tf_op jit(solution)/shard_map/ppermute | solution.py:15
  22.1 5.6 %collective-permute-start.2 = (bf16[2,128,128]{2,1,0:T(8,128)(2,1)S(1)}, bf16[2,128,128]{2,1,0:T(8,128)(2,1)S(1)}, u32[]{:S(2)}, u32[]{:S(2)}) collective-permute-start(bf16[2,128,128]{2,1,0:T(8,128)(2,1)S(1)} %add_convert_fusion.5), channel_id=1, source_target_pairs={{0,32},{32,64},{64,96},{96,128},{128,160},{160,192},{192,224},{1,3... | collective-permute-start | bytes 196616 | tf_op jit(solution)/shard_map/ppermute | solution.py:15
  27.8 5.6 %collective-permute-start.3 = (bf16[2,128,128]{2,1,0:T(8,128)(2,1)S(1)}, bf16[2,128,128]{2,1,0:T(8,128)(2,1)S(1)}, u32[]{:S(2)}, u32[]{:S(2)}) collective-permute-start(bf16[2,128,128]{2,1,0:T(8,128)(2,1)S(1)} %add_convert_fusion.4), channel_id=1, source_target_pairs={{0,32},{32,64},{64,96},{96,128},{128,160},{160,192},{192,224},{1,3... | collective-permute-start | bytes 196616 | tf_op jit(solution)/shard_map/ppermute | solution.py:15
  33.5 5.6 %collective-permute-start.4 = (bf16[2,128,128]{2,1,0:T(8,128)(2,1)S(1)}, bf16[2,128,128]{2,1,0:T(8,128)(2,1)S(1)}, u32[]{:S(2)}, u32[]{:S(2)}) collective-permute-start(bf16[2,128,128]{2,1,0:T(8,128)(2,1)S(1)} %add_convert_fusion.3), channel_id=1, source_target_pairs={{0,32},{32,64},{64,96},{96,128},{128,160},{160,192},{192,224},{1,3... | collective-permute-start | bytes 196616 | tf_op jit(solution)/shard_map/ppermute | solution.py:15
  39.1 5.6 %collective-permute-start.5 = (bf16[2,128,128]{2,1,0:T(8,128)(2,1)S(1)}, bf16[2,128,128]{2,1,0:T(8,128)(2,1)S(1)}, u32[]{:S(2)}, u32[]{:S(2)}) collective-permute-start(bf16[2,128,128]{2,1,0:T(8,128)(2,1)S(1)} %add_convert_fusion.2), channel_id=1, source_target_pairs={{0,32},{32,64},{64,96},{96,128},{128,160},{160,192},{192,224},{1,3... | collective-permute-start | bytes 196616 | tf_op jit(solution)/shard_map/ppermute | solution.py:15
  44.8 5.6 %collective-permute-start.6 = (bf16[2,128,128]{2,1,0:T(8,128)(2,1)S(1)}, bf16[2,128,128]{2,1,0:T(8,128)(2,1)S(1)}, u32[]{:S(2)}, u32[]{:S(2)}) collective-permute-start(bf16[2,128,128]{2,1,0:T(8,128)(2,1)S(1)} %add_convert_fusion.1), channel_id=1, source_target_pairs={{0,32},{32,64},{64,96},{96,128},{128,160},{160,192},{192,224},{1,3... | collective-permute-start | bytes 196616 | tf_op jit(solution)/shard_map/ppermute | solution.py:15
  51.0 1.9 copy-start.8
  52.8 207.9 %all-gather.2.cloned.1.call-start = ((), (), s32[]{:S(2)}) async-start(), calls=%async_computation.3 | async-start | bytes 8847360 | tf_op jit(solution)/shard_map/all_gather | solution.py:105
  61.4 0.5 copy-start.10
  207.3 4.8 copy-start.2
  207.3 4.8 copy-start.3
  207.3 4.8 copy-start.7
  214.1 108.7 %reduce-scatter.5.cloned.1.call-start = ((), (), s32[]{:S(2)}) async-start(), calls=%async_computation.4 | async-start | bytes 8847360 | tf_op jit(solution)/shard_map/reduce_scatter | solution.py:114
  260.7 5.4 copy-start.5
  271.5 2.7 copy-start.9
  271.5 2.7 copy-start.11
  271.5 272.7 %reduce-scatter.7.cloned.1.call-start = ((), (), s32[]{:S(2)}) async-start(), calls=%async_computation.5 | async-start | bytes 1622016
  (1 other events, 0.5 us)
Sparse Core Ops, SparseCore 0:
  52.9 154.3 all-reduce.1
  214.2 46.4 all-gather.1
  271.6 51.0 reduce-scatter.4
  327.0 217.1 reduce-scatter.6
where the time goes:
time: 556 us
  waiting for transfers between devices  481 us (87%)
  matrix products  25 us (4%)
  starting transfers between devices  13.6 us (2%)
  between operations  13.4 us (2%)
  local copies, waits for them, and re-layouts  12.3 us (2%)
  other arithmetic  10.6 us (2%)
    unnamed x5, waiting for transfers between devices  217 us
    psum x1, waiting for transfers between devices, local(): lax.psum(jnp.dot(attn_heads, w_out, preferred_element_type=jnp.float32).a...  145 us
    reduce_scatter x1, waiting for transfers between devices, local(): lax.psum_scatter(partials.astype(jnp.float32).astype(jnp.bfloat16), 'ctx'...  47.8 us
    all_gather x1, waiting for transfers between devices, local(): lax.all_gather(slot_buffer, 'ctx', axis=0, tiled=True)  46.6 us
    ppermute x7, waiting for transfers between devices, shifted(): lax.ppermute(value, axis, [(source, source + steps) for source in range(i...  23.4 us
    ppermute x7, starting transfers between devices, shifted(): lax.ppermute(value, axis, [(source, source + steps) for source in range(i...  13.4 us
  transfers between devices with their start and end apart: 11, of which 11 were waited for; matrix products, arithmetic and copies ran while one was open for 3% of the time, Pallas kernels for 0%

commit v1 on v0

--- a/solution.py
+++ b/solution.py
@@ -102,7 +102,9 @@
     )
     combine = jnp.sum(jnp.where(in_slot, gates[:, :, None], 0.0), axis=1)
     projected = lax.dot_general(
-        lax.all_gather(slot_buffer, "ctx", axis=0, tiled=True),
+        jnp.concatenate(
+            lax.all_to_all(jnp.stack([slot_buffer] * lax.axis_size("ctx")), "ctx", 0, 0), axis=0
+        ),
         paired,
         (((1,), (1,)), ((), ())),
         preferred_element_type=jnp.float32,

time: 556 us -> 596 us (1.072)
  blocking collectives: 0 us -> 93.4 us
  waiting for transfers between devices: 481 us -> 429 us
    all_to_all x0 -> x1, blocking collectives: none -> 93.4 us  [local(): lax.all_to_all(jnp.stack([slot_buffer] * lax.axis_size('ctx')), 'ctx', 0, 0)]
    all_gather x1 -> x0, waiting for transfers between devices: 46.6 us -> none  [local(): lax.all_gather(slot_buffer, 'ctx', axis=0, tiled=True)]
    unnamed x5 -> x4, waiting for transfers between devices: 217 us -> 217 us
  transfers between devices with their start and end apart: 11 -> 10, of which waited for: 11 -> 10; matrix products, arithmetic and copies ran while one was open for 3% -> 2% of each run, Pallas kernels for 0% -> 0%
where the time goes in v1:
time: 596 us; the launch traced here: 595 us
  waiting for transfers between devices  429 us (72%)
  blocking collectives  93.4 us (16%)
  matrix products  21.5 us (4%)
  starting transfers between devices  13.7 us (2%)
  between operations  13.4 us (2%)
  local copies, waits for them, and re-layouts  13.3 us (2%)
  other arithmetic  10.6 us (2%)
    unnamed x4, waiting for transfers between devices  217 us
    psum x1, waiting for transfers between devices, local(): lax.psum(jnp.dot(attn_heads, w_out, preferred_element_type=jnp.float32).a...  145 us
    all_to_all x1, blocking collectives, local(): lax.all_to_all(jnp.stack([slot_buffer] * lax.axis_size('ctx')), 'ctx', 0, 0)  93.4 us
    reduce_scatter x1, waiting for transfers between devices, local(): lax.psum_scatter(partials.astype(jnp.float32).astype(jnp.bfloat16), 'ctx'...  43 us
    ppermute x7, waiting for transfers between devices, shifted(): lax.ppermute(value, axis, [(source, source + steps) for source in range(i...  23.4 us
    ppermute x7, starting transfers between devices, shifted(): lax.ppermute(value, axis, [(source, source + steps) for source in range(i...  13.4 us
  transfers between devices with their start and end apart: 10, of which 10 were waited for; matrix products, arithmetic and copies ran while one was open for 2% of the time, Pallas kernels for 0%

profile of v1, /device:TPU:2, one launch (start us, length us, event | category | flops | bytes accessed | tf_op | source)
XLA Modules:
  0.0 595.0 jit_solution(18327666043087606527)
XLA Ops:
  10.8 1.9 collective-permute-start
  12.7 3.7 collective-permute-done
  16.4 1.9 collective-permute-start.1
  18.4 3.7 collective-permute-done.1
  22.1 1.9 collective-permute-start.2
  24.0 3.7 collective-permute-done.2
  27.8 1.9 collective-permute-start.3
  29.7 3.7 collective-permute-done.3
  33.5 1.9 collective-permute-start.4
  35.4 3.6 collective-permute-done.4
  39.1 1.9 collective-permute-start.5
  42.1 2.6 collective-permute-done.5
  44.8 1.9 collective-permute-start.6
  47.9 2.5 collective-permute-done.6
  51.0 1.8 convolution_convert_fusion.2
  61.9 145.4 %all-reduce.2.cloned.1.call-done = bf16[128,6144]{1,0:T(8,128)(2,1)} async-done(((bf16[128,6144]{1,0:T(8,128)(2,1)}), bf16[128,6144]{1,0:T(8,128)(2,1)}) %all-reduce.2.cloned.1.call-update) | async-done | bytes 1572880 | tf_op jit(solution)/shard_map/psum | solution.py:76
  207.3 4.3 multiply_reduce_fusion
  214.0 93.4 %all_to_all.5 = bf16[8,80,6144]{2,1,0:T(8,128)(2,1)S(1)} all-to-all(bf16[8,80,6144]{2,1,0:T(8,128)(2,1)S(1)} %stack.2), channel_id=1, replica_groups=mesh['ctx'=8,'exp'=32] {'ctx'}, dimensions={0} | all-to-all | bytes 15728640 | tf_op jit(solution)/shard_map/all_to_all | solution.py:106
  307.3 2.9 fusion.31
  310.3 5.4 convolution_convert_fusion
  315.9 2.6 fusion.30
  319.2 43.0 %reduce-scatter.5.cloned.1.call-done = bf16[80,6144]{1,0:T(8,128)(2,1)} async-done(((bf16[640,6144]{1,0:T(8,128)(2,1)}), bf16[80,6144]{1,0:T(8,128)(2,1)}) %reduce-scatter.5.cloned.1.call-update) | async-done | bytes 983056 | tf_op jit(solution)/shard_map/reduce_scatter | solution.py:116
  362.2 4.1 fusion
  366.4 217.4 %reduce-scatter.7.cloned.1.call-done = bf16[192,128]{1,0:T(8,128)(2,1)} async-done(((bf16[6144,128]{1,0:T(8,128)(2,1)}), bf16[192,128]{1,0:T(8,128)(2,1)}) %reduce-scatter.7.cloned.1.call-update) | async-done | bytes 49168
  (78 shorter events, 24.6 us)
Async XLA Ops:
  6.5 300.8 %copy-start = (bf16[2,144,6144]{2,1,0:T(8,128)(2,1)S(1)}, bf16[2,144,6144]{2,1,0:T(8,128)(2,1)}, u32[]{:S(2)}) copy-start(bf16[2,144,6144]{2,1,0:T(8,128)(2,1)} %param.24) | copy-start | bytes 10616836
  6.5 200.8 %all-reduce.2.cloned.1.call-start = ((), (), s32[]{:S(2)}) async-start(), calls=%async_computation.3 | async-start | bytes 3145728 | tf_op jit(solution)/shard_map/psum | solution.py:76
  9.5 40.9 %copy-start.1 = (f32[2,128,128]{2,1,0:T(8,128)S(1)}, f32[2,128,128]{2,1,0:T(8,128)}, u32[]{:S(2)}) copy-start(f32[2,128,128]{2,1,0:T(8,128)} %param.18) | copy-start | bytes 393220
  9.5 40.9 %copy-start.6 = (bf16[128,256]{1,0:T(8,128)(2,1)S(1)}, bf16[128,256]{1,0:T(8,128)(2,1)}, u32[]{:S(2)}) copy-start(bf16[128,256]{1,0:T(8,128)(2,1)} %param.14) | copy-start | bytes 196612
  9.5 41.4 %copy-start.12 = (f32[256]{0:T(256)S(1)}, f32[256]{0:T(256)}, u32[]{:S(2)}) copy-start(f32[256]{0:T(256)} %param.19) | copy-start | bytes 3076
  9.5 41.5 %copy-start.4 = (bf16[256,6144]{1,0:T(8,128)(2,1)S(1)}, bf16[256,6144]{1,0:T(8,128)(2,1)}, u32[]{:S(2)}) copy-start(bf16[256,6144]{1,0:T(8,128)(2,1)} %param.20) | copy-start | bytes 9437188
  10.8 5.6 collective-permute-start
  16.4 5.6 collective-permute-start.1
  22.1 5.6 collective-permute-start.2
  27.8 5.6 collective-permute-start.3
  33.5 5.6 collective-permute-start.4
  39.1 5.6 collective-permute-start.5
  44.8 5.6 collective-permute-start.6
  51.0 1.9 copy-start.8
  52.8 309.4 %reduce-scatter.5.cloned.1.call-start = ((), (), s32[]{:S(2)}) async-start(), calls=%async_computation.4 | async-start | bytes 8847360 | tf_op jit(solution)/shard_map/reduce_scatter | solution.py:116
  61.3 0.5 copy-start.10
  207.3 4.8 copy-start.2
  207.3 4.8 copy-start.3
  207.3 4.8 copy-start.7
  211.6 0.5 copy-start.13
  307.3 2.9 copy-start.5
  315.7 2.9 copy-start.9
  315.7 2.9 copy-start.11
  315.7 268.1 %reduce-scatter.7.cloned.1.call-start = ((), (), s32[]{:S(2)}) async-start(), calls=%async_computation.5 | async-start | bytes 1622016
Sparse Core Ops, SparseCore 0:
  52.9 154.3 all-reduce.1
  315.8 46.3 reduce-scatter.4
  366.5 217.1 reduce-scatter.6
